TPU v7x, 256 devices: a whole 4x4x8 slice. The times are simulated.
256 devices in a mesh: tp: 8 (over z), ep: 32 (over x, y, core).
Axes of the slice: x: 4, y: 4, z: 8, core: 2. Of those that a mesh axis runs over, the one named last changes fastest.
Arguments:
- tokens: bfloat16 [8192, 2048], P('ep'), may hold values from -6 to 6
- expert_ids: int32 [8192, 8], P('ep'), may hold values from 0 to 127, all different within a row; in each aligned block of 256 rows (0 to 255, 256 to 511, ...) at most 24 rows name the same one
- gate_weights: float32 [8192, 8], P('ep'), may hold values from 0.02 to 0.3
- grad_output: bfloat16 [8192, 2048], P('ep'), may hold values from -6 to 6
- w_gate_up: bfloat16 [256, 2048, 768], P(('tp', 'ep')), may hold values from -0.125 to 0.125
- w_down: bfloat16 [256, 384, 2048], P(('tp', 'ep')), may hold values from -0.21875 to 0.21875
Outputs:
- mixed: bfloat16 [8192, 2048], P('ep', 'tp')
- grad_tokens: bfloat16 [8192, 2048], P('ep', 'tp')
- grad_gates: float32 [8192, 8], P('ep', 'tp')
- grad_w_gate_up: bfloat16 [256, 2048, 768], P(('tp', 'ep'))
- grad_w_down: bfloat16 [256, 384, 2048], P(('tp', 'ep'))
Inputs may be any that keep to these rules, and one draw needn't show every extreme that they name: `expert_ids`: each row names 8 different experts. Among the 256 rows of one index of ep no expert is named more than 24 times, and in every draw some expert is named exactly 24 times there.
All inputs are finite; a program needn't handle non-finite values.
Results may differ from a plain program's by a relative error of at most 0.012.
Values may be sent and summed in bfloat16 or wider, within the bound.
A program may use at most 128 MiB of HBM per device.

v0:
```python
import functools

import jax
import jax.numpy as jnp
from jax import lax
from jax.experimental import pallas as pl
from jax.experimental.pallas import tpu as pltpu
from jax.sharding import PartitionSpec as P

MESH = pl.DeviceIdType.MESH
F32 = jnp.float32
BF16 = jnp.bfloat16
NX, NY, NC, NZ = 4, 4, 2, 8
OFFS = (1, 3, 2)
TOK, TOP, WIDTH, CAP, FFP = 256, 8, 2048, 24, 384
EXP = NX * NY
SLOTS = EXP * CAP
BLK = WIDTH // NZ
IN_CHUNKS = ((0, 512), (512, 512), (1024, 512), (1536, 512))
OUT_CHUNKS = ((0, 0, 5), (1, 0, 5), (0, 5, 3), (1, 5, 3))
NN = (((1,), (0,)), ((), ()))
NT = (((1,), (1,)), ((), ()))
TN = (((0,), (0,)), ((), ()))


def dot(a, b, dims=NN):
    return lax.dot_general(a, b, dims, preferred_element_type=F32)


def ring_step(pos):
    far = 3 - (pos - 1) // 2
    return jnp.where(pos == 0, 4, jnp.where(pos % 2 == 1, far, -far))


def kernel(
    tok, ids, gates, gout, wgu_in, wd_in,
    mixed_o, gtok_o, gg_o, gwgu_o, gwd_o,
    wgu, wd, send, mid, fin, rmid, rfin, rows2, act, dpre, pre, dact, onehot, comb,
    terms, zpart, zs, zr, gsend, gin, gst_gu, gst_d,
    w_ls, w_ss, w_rs, a_ss, a_rs, a_ls, p_ss, p_rs, z_ss, z_rs, g_ss, g_rs, o_s,
):
    z = lax.axis_index("tp")
    ep = lax.axis_index("ep")
    x, y, c = ep // (NY * NC), (ep // NC) % NY, ep % NC

    def dev(zz, xx, yy, cc):
        return (zz, (xx * NY + yy) * NC + cc)

    other = dev(z, x, y, 1 - c)
    own_rows = pl.multiple_of(c * SLOTS, SLOTS)

    def remote(src, dst, ss, rs, to):
        return pltpu.make_async_remote_copy(
            src_ref=src, dst_ref=dst, send_sem=ss, recv_sem=rs, device_id=to, device_id_type=MESH
        )

    w_local = [
        pltpu.make_async_copy(wgu_in.at[0], wgu.at[c], w_ls.at[0]),
        pltpu.make_async_copy(wd_in.at[0], wd.at[c], w_ls.at[1]),
    ]
    for cp in w_local:
        cp.start()
    w_out = [
        remote(wgu_in.at[0], wgu.at[c], w_ss.at[0], w_rs.at[0], other),
        remote(wd_in.at[0], wd.at[c], w_ss.at[1], w_rs.at[1], other),
    ]
    w_come = [
        remote(wgu_in.at[0], wgu.at[1 - c], w_ss.at[0], w_rs.at[0], other),
        remote(wd_in.at[0], wd.at[1 - c], w_ss.at[1], w_rs.at[1], other),
    ]

    barrier = pltpu.get_barrier_semaphore()
    peers = [dev(z, (x + d) % NX, y, c) for d in OFFS]
    peers += [dev(z, x, (y + d) % NY, c) for d in OFFS]
    peers += [dev((z + d) % NZ, x, y, c) for d in range(1, NZ)]
    peers += [other]
    for peer in peers:
        pl.semaphore_signal(barrier, inc=1, device_id=peer, device_id_type=MESH)

    local_ids = ids[...] - z * EXP
    hits, gate_rows = [], []
    for e in range(EXP):
        hit = jnp.where(local_ids == e, 1.0, 0.0)
        hits.append(jnp.sum(hit, axis=0, keepdims=True))
        gate_rows.append(jnp.sum(hit * gates[...], axis=0, keepdims=True))
    hit_all = jnp.concatenate(hits, axis=0)
    before = lax.broadcasted_iota(jnp.int32, (TOK, TOK), 0) < lax.broadcasted_iota(jnp.int32, (TOK, TOK), 1)
    rank = dot(hit_all.astype(BF16), jnp.where(before, 1.0, 0.0).astype(BF16))
    slot = lax.broadcasted_iota(jnp.int32, (CAP, TOK), 0).astype(F32)
    slot_gates = []
    for e in range(EXP):
        chosen = jnp.where(slot == rank[e : e + 1], hits[e], 0.0)
        onehot[e * CAP : (e + 1) * CAP, :] = chosen
        slot_gates.append(jnp.sum(chosen * gate_rows[e], axis=1, keepdims=True))
    slot_gate = jnp.concatenate(slot_gates, axis=0)
    picks = onehot[...].astype(BF16)

    def exchange(n, src, mid_ref, fin_ref, cols, x_first):
        col = slice(None) if cols is None else pl.ds(*cols)

        def part(ref, i, along_x):
            return ref.at[i, :, :, col] if along_x else ref.at[:, i, :, col]

        def phase(k, frm, into, along_x):
            here = x if along_x else y
            out, come = [], []
            for m, d in enumerate(OFFS):
                to, back = (here + d) % 4, (here + 4 - d) % 4
                place = dev(z, to, y, c) if along_x else dev(z, x, to, c)
                sems = (a_ss.at[n, k * 3 + m], a_rs.at[n, k * 3 + m])
                out.append(remote(part(frm, to, along_x), part(into, here, along_x), *sems, place))
                come.append(remote(part(frm, to, along_x), part(into, back, along_x), *sems, place))
            stay = pltpu.make_async_copy(part(frm, here, along_x), part(into, here, along_x), a_ls.at[n, k])
            return out, come, stay

        first = phase(0, src, mid_ref, x_first)
        second = phase(1, mid_ref, fin_ref, not x_first)

        def start(ph):
            for cp in ph[0]:
                cp.start()
            ph[2].start()

        def arrive(ph):
            for cp in ph[1]:
                cp.wait_recv()
            ph[2].wait()

        def forward():
            arrive(first)
            start(second)

        def sent(ph):
            for cp in ph[0]:
                cp.wait_send()

        return dict(
            start=lambda: start(first),
            forward=forward,
            arrive=lambda: arrive(second),
            sent1=lambda: sent(first),
            sent2=lambda: sent(second),
        )

    def stacked(value):
        return value.astype(F32).reshape(SLOTS, value.shape[-1]).astype(BF16)

    def unstacked(value):
        return value.reshape(NX, NY, CAP, value.shape[-1]).astype(BF16)

    incoming = []
    for n, cols in enumerate(IN_CHUNKS):
        incoming.append(
            [exchange(2 * n + a, send.at[a], mid.at[a], fin.at[a], cols, a == 0) for a in range(2)]
        )

    def gather(n):
        at, many = IN_CHUNKS[n]
        send[0, :, :, :, at : at + many] = unstacked(dot(picks, tok[:, at : at + many]))
        send[1, :, :, :, at : at + many] = unstacked(dot(picks, gout[:, at : at + many]) * slot_gate)

    def begin(n):
        for ex in incoming[n]:
            ex["start"]()

    def forward_in(n):
        for ex in incoming[n]:
            ex["forward"]()

    def first_part(n):
        at, many = IN_CHUNKS[n]
        for ex in incoming[n]:
            ex["arrive"]()
        for a in range(2):
            rows2[a, pl.ds(own_rows, SLOTS), at : at + many] = stacked(fin[a, :, :, :, at : at + many])

        def half(h, carry):
            new_pre = dot(rows2[0, pl.ds(own_rows, SLOTS), at : at + many], wgu[h, at : at + many, :])
            new_dact = dot(rows2[1, pl.ds(own_rows, SLOTS), at : at + many], wd[h, :, at : at + many], NT)
            if n > 0:
                new_pre = new_pre + pre[h]
                new_dact = new_dact + dact[h]
            if n < len(IN_CHUNKS) - 1:
                pre[h] = new_pre
                dact[h] = new_dact
            else:
                g, u = new_pre[:, :FFP], new_pre[:, FFP:]
                sigma = jax.nn.sigmoid(g)
                act[h, pl.ds(own_rows, SLOTS), :] = (g * sigma * u).astype(BF16)
                dpre[h, pl.ds(own_rows, SLOTS), :FFP] = (
                    new_dact * u * sigma * (1.0 + g * (1.0 - sigma))
                ).astype(BF16)
                dpre[h, pl.ds(own_rows, SLOTS), FFP:] = (new_dact * g * sigma).astype(BF16)
            return carry

        lax.fori_loop(0, 2, half, 0)

    gather(0)
    pl.semaphore_wait(barrier, len(peers))
    begin(0)
    for cp in w_out:
        cp.start()
    gather(1)
    begin(1)
    gather(2)
    forward_in(0)
    begin(2)
    gather(3)
    comb[1] = onehot[...].T.astype(BF16)
    comb[0] = (onehot[...] * slot_gate).T.astype(BF16)
    forward_in(1)
    begin(3)
    for cp in w_local:
        cp.wait()
    for cp in w_come:
        cp.wait_recv()
    forward_in(2)
    first_part(0)
    forward_in(3)
    first_part(1)
    first_part(2)
    for pair in incoming:
        for ex in pair:
            ex["sent1"]()
    first_part(3)

    pushes = [
        (rows2.at[0], own_rows),
        (rows2.at[1], own_rows),
        (act.at[1 - c], own_rows),
        (dpre.at[1 - c], own_rows),
    ]
    lands = [rows2.at[0], rows2.at[1], act.at[c], dpre.at[c]]
    their_rows = pl.multiple_of((1 - c) * SLOTS, SLOTS)
    push_out = [
        remote(r.at[pl.ds(at, SLOTS)], r.at[pl.ds(at, SLOTS)], p_ss.at[i], p_rs.at[i], other)
        for i, (r, at) in enumerate(pushes)
    ]
    push_come = [
        remote(r.at[pl.ds(their_rows, SLOTS)], r.at[pl.ds(their_rows, SLOTS)], p_ss.at[i], p_rs.at[i], other)
        for i, r in enumerate(lands)
    ]

    outgoing = []
    for n, (a, at, many) in enumerate(OUT_CHUNKS):
        half = many * BLK // 2
        base = 8 + 2 * n
        outgoing.append(
            [
                exchange(base + i, send.at[a], rmid.at[a], rfin.at[a], (at * BLK + i * half, half), i == 0)
                for i in range(2)
            ]
        )

    def plane_cols(pos):
        return pl.multiple_of(((z + ring_step(pos) + NZ) % NZ) * BLK, BLK)

    def second_part(n):
        a, at, many = OUT_CHUNKS[n]

        def block(pos, carry):
            j = plane_cols(pos)
            if a == 0:
                total = dot(act[0, pl.ds(own_rows, SLOTS), :], wd[0, :, pl.ds(j, BLK)])
                total += dot(act[1, pl.ds(own_rows, SLOTS), :], wd[1, :, pl.ds(j, BLK)])
            else:
                total = dot(dpre[0, pl.ds(own_rows, SLOTS), :], wgu[0, pl.ds(j, BLK), :], NT)
                total += dot(dpre[1, pl.ds(own_rows, SLOTS), :], wgu[1, pl.ds(j, BLK), :], NT)
            send[a, :, :, :, pl.ds(pl.multiple_of(pos * BLK, BLK), BLK)] = unstacked(total)
            return carry

        lax.fori_loop(at, at + many, block, 0)
        for ex in outgoing[n]:
            ex["start"]()

    def forward_out(n):
        for ex in outgoing[n]:
            ex["forward"]()

    def combine(n):
        a, at, many = OUT_CHUNKS[n]
        for ex in outgoing[n]:
            ex["arrive"]()

        def block(pos, carry):
            r = stacked(rfin[a, :, :, :, pl.ds(pl.multiple_of(pos * BLK, BLK), BLK)])
            zpart[a, pos] = dot(comb[a], r)
            if a == 0:
                terms[...] += dot(r, gout[:, pl.ds(plane_cols(pos), BLK)], NT)
            return carry

        lax.fori_loop(at, at + many, block, 0)

    ring_pos = (0, 1, 3, 5, 2, 4, 6)

    def ring_copy(a, m):
        to = dev((z + (1 if m < 4 else NZ - 1)) % NZ, x, y, c)
        return remote(zs.at[a, m], zr.at[a, m], z_ss.at[a, m], z_rs.at[a, m], to)

    def ring(a, m):
        total = zpart[a, ring_pos[m]]
        if m not in (0, 4):
            ring_copy(a, m - 1).wait_recv()
            total = total + zr[a, m - 1].astype(F32)
        zs[a, m] = total.astype(BF16)
        ring_copy(a, m).start()

    def ring_end(a, out):
        ring_copy(a, 3).wait_recv()
        ring_copy(a, 6).wait_recv()
        out[...] = (zpart[a, 7] + zr[a, 3].astype(F32) + zr[a, 6].astype(F32)).astype(BF16)

    out_copies = []

    def grad_gu(lo, hi):
        def tile(i, carry):
            cols = pl.ds(pl.multiple_of(i * 256, 256), 256)
            gst_gu[cols, :] = dot(rows2[0, :, cols], dpre[c], TN).astype(BF16)
            return carry

        lax.fori_loop(lo, hi, tile, 0)
        part = pl.ds(lo * 256, (hi - lo) * 256)
        cp = pltpu.make_async_copy(gst_gu.at[part], gwgu_o.at[0, part], o_s.at[len(out_copies)])
        cp.start()
        out_copies.append(cp)

    def grad_d(lo, hi):
        def tile(i, carry):
            cols = pl.ds(pl.multiple_of(i * 512, 512), 512)
            gst_d[:, cols] = dot(act[c], rows2[1, :, cols], TN).astype(BF16)
            return carry

        lax.fori_loop(lo, hi, tile, 0)
        part = pl.ds(lo * 512, (hi - lo) * 512)
        cp = pltpu.make_async_copy(gst_d.at[:, part], gwd_o.at[0, :, part], o_s.at[len(out_copies)])
        cp.start()
        out_copies.append(cp)

    second_part(0)
    second_part(1)
    for cp in push_out:
        cp.start()
    forward_out(0)
    second_part(2)
    second_part(3)
    terms[...] = jnp.zeros_like(terms)
    forward_out(1)
    for cp in push_come:
        cp.wait_recv()
    grad_gu(0, 2)
    combine(0)
    ring(0, 0)
    ring(0, 4)
    forward_out(2)
    grad_gu(2, 4)
    ring(0, 1)
    ring(0, 5)
    combine(1)
    ring(1, 0)
    ring(1, 4)
    ring(0, 2)
    forward_out(3)
    grad_gu(4, 6)
    ring(1, 1)
    ring(1, 5)
    grad_gu(6, 8)
    ring(1, 2)
    grad_d(0, 2)
    combine(2)
    ring(0, 3)
    ring(0, 6)

    kept = terms[...] * onehot[...]
    total = jnp.zeros((TOP, TOK), F32)
    for e in range(EXP):
        value = jnp.sum(kept[e * CAP : (e + 1) * CAP], axis=0, keepdims=True)
        total += jnp.where(local_ids == e, value, 0.0)
    for k in range(TOP):
        gsend[k] = jnp.broadcast_to(total[k : k + 1], (8, TOK))
    g_out, g_come = [], []
    for d in range(1, NZ):
        j, back = (z + d) % NZ, (z + NZ - d) % NZ
        sems = (g_ss.at[d - 1], g_rs.at[d - 1])
        g_out.append(remote(gsend.at[j], gin.at[z], *sems, dev(j, x, y, c)))
        g_come.append(remote(gsend.at[j], gin.at[back], *sems, dev(j, x, y, c)))
    for cp in g_out:
        cp.start()
    gin[z] = gsend[z]
    grad_d(2, 4)

    combine(3)
    ring(1, 3)
    ring(1, 6)
    ring_end(0, mixed_o)
    for cp in g_come:
        cp.wait_recv()
    gg_o[...] = jnp.sum(gin[...], axis=0)
    ring_end(1, gtok_o)

    for cp in w_out:
        cp.wait_send()
    for pair in incoming:
        for ex in pair:
            ex["sent2"]()
    for cp in push_out:
        cp.wait_send()
    for pair in outgoing:
        for ex in pair:
            ex["sent1"]()
            ex["sent2"]()
    for a in range(2):
        for m in range(7):
            ring_copy(a, m).wait_send()
    for cp in g_out:
        cp.wait_send()
    for cp in out_copies:
        cp.wait()


def local(tokens, expert_ids, gate_weights, grad_output, w_gate_up, w_down):
    vmem = pl.BlockSpec(memory_space=pltpu.VMEM)
    hbm = pl.BlockSpec(memory_space=pl.ANY)
    dma = pltpu.SemaphoreType.DMA
    quads = (2, NX, NY, CAP, WIDTH)
    mixed, grad_tokens, gates, grad_gu, grad_dn = pl.pallas_call(
        kernel,
        out_shape=(
            jax.ShapeDtypeStruct((TOK, BLK), BF16),
            jax.ShapeDtypeStruct((TOK, BLK), BF16),
            jax.ShapeDtypeStruct((8, TOK), F32),
            jax.ShapeDtypeStruct(w_gate_up.shape, BF16),
            jax.ShapeDtypeStruct(w_down.shape, BF16),
        ),
        in_specs=[vmem, vmem, vmem, vmem, hbm, hbm],
        out_specs=(vmem, vmem, vmem, hbm, hbm),
        scratch_shapes=[
            pltpu.VMEM((2, WIDTH, 2 * FFP), BF16),
            pltpu.VMEM((2, FFP, WIDTH), BF16),
            pltpu.VMEM(quads, BF16),
            pltpu.VMEM(quads, BF16),
            pltpu.VMEM(quads, BF16),
            pltpu.VMEM(quads, BF16),
            pltpu.VMEM(quads, BF16),
            pltpu.VMEM((2, NC * SLOTS, WIDTH), BF16),
            pltpu.VMEM((2, NC * SLOTS, FFP), BF16),
            pltpu.VMEM((2, NC * SLOTS, 2 * FFP), BF16),
            pltpu.VMEM((2, SLOTS, 2 * FFP), F32),
            pltpu.VMEM((2, SLOTS, FFP), F32),
            pltpu.VMEM((SLOTS, TOK), F32),
            pltpu.VMEM((2, TOK, SLOTS), BF16),
            pltpu.VMEM((SLOTS, TOK), F32),
            pltpu.VMEM((2, NZ, TOK, BLK), F32),
            pltpu.VMEM((2, 7, TOK, BLK), BF16),
            pltpu.VMEM((2, 7, TOK, BLK), BF16),
            pltpu.VMEM((TOP, 8, TOK), F32),
            pltpu.VMEM((NZ, 8, TOK), F32),
            pltpu.VMEM((WIDTH, 2 * FFP), BF16),
            pltpu.VMEM((FFP, WIDTH), BF16),
            dma((2,)), dma((2,)), dma((2,)),
            dma((16, 6)), dma((16, 6)), dma((16, 2)),
            dma((4,)), dma((4,)),
            dma((2, 7)), dma((2, 7)),
            dma((7,)), dma((7,)),
            dma((6,)),
        ],
        compiler_params=pltpu.CompilerParams(
            collective_id=0, has_side_effects=True, vmem_limit_bytes=63 * 1024 * 1024
        ),
        name="moe",
    )(tokens, expert_ids.T, gate_weights.T, grad_output, w_gate_up, w_down)
    return mixed, grad_tokens, gates[:1].T, grad_gu, grad_dn


def solution(mesh):
    placed = (
        P("ep", None),
        P("ep", None),
        P("ep", None),
        P("ep", None),
        P(("tp", "ep"), None, None),
        P(("tp", "ep"), None, None),
    )
    return jax.shard_map(
        local,
        mesh=mesh,
        in_specs=placed,
        out_specs=(
            P("ep", "tp"),
            P("ep", "tp"),
            P("ep", "tp"),
            P(("tp", "ep"), None, None),
            P(("tp", "ep"), None, None),
        ),
        check_vma=False,
    )
```

profile of v0, /device:TPU:2, one launch (start us, length us, event | category | flops | bytes accessed | tf_op | source)
XLA Modules:
  0.0 114.9 jit_solution(3616999974107468168)
XLA Ops:
  0.6 104.9 %moe.1 = (bf16[256,256]{1,0:T(8,128)(2,1)}, bf16[256,256]{1,0:T(8,128)(2,1)}, f32[8,256]{1,0:T(8,128)}, bf16[1,2048,768]{2,1,0:T(8,128)(2,1)}, bf16[1,384,2048]{2,1,0:T(8,128)(2,1)}) custom-call(bf16[256,2048]{1,0:T(8,128)(2,1)} %tok.1, s32[8,256]{1,0:T(8,128)} %bitcast.4, f32[8,256]{1,0:T(8,128)} %bitcast.5, bf16[256,2048]{1,0:T(8,128)(2,1)} %gout.1, ...), custom_call_target="tpu_custom_call" | custom-call | tf_op jit(solution)/shard_map/moe/pallas_call | solution.py:425
  105.5 1.3 %slice_bitcast_fusion = f32[256,1]{0,1:T(1,128)} fusion(f32[8,256]{1,0:T(8,128)} %get-tuple-element.12), kind=kLoop, calls=%fused_computation | loop fusion | bytes 2048 | tf_op jit(solution)/shard_map/transpose | solution.py:471
  106.8 1.6 %copy.15 = bf16[256,256]{1,0:T(8,128)(2,1)} copy(bf16[256,256]{1,0:T(8,128)(2,1)} %get-tuple-element.20) | data formatting | bytes 262144
  108.3 1.6 %copy.16 = bf16[256,256]{1,0:T(8,128)(2,1)} copy(bf16[256,256]{1,0:T(8,128)(2,1)} %get-tuple-element.21) | data formatting | bytes 262144
  109.9 0.0 copy-start
  109.9 3.9 %copy.17 = bf16[1,2048,768]{2,1,0:T(8,128)(2,1)} copy(bf16[1,2048,768]{2,1,0:T(8,128)(2,1)} %get-tuple-element.23) | data formatting | bytes 6291456
  113.8 0.0 copy-done
  113.8 1.1 copy.18
Async XLA Ops:
  109.9 3.9 %copy-start = (bf16[1,384,2048]{2,1,0:T(8,128)(2,1)S(1)}, bf16[1,384,2048]{2,1,0:T(8,128)(2,1)}, u32[]{:S(2)}) copy-start(bf16[1,384,2048]{2,1,0:T(8,128)(2,1)} %get-tuple-element.24) | copy-start | bytes 4718596
where the time goes:
time: 115 us
  Pallas kernels  105 us (91%)
  local copies, waits for them, and re-layouts  9.41 us (8%)
    pallas_call x1, Pallas kernels, local(): pl.pallas_call(kernel, out_shape=(jax.ShapeDtypeStruct((TOK, BLK), BF16),...  105 us
    unnamed x6, local copies, waits for them, and re-layouts  8.15 us

commit v1 on v0

--- a/solution.py
+++ b/solution.py
@@ -16,8 +16,17 @@
 EXP = NX * NY
 SLOTS = EXP * CAP
 BLK = WIDTH // NZ
-IN_CHUNKS = ((0, 512), (512, 512), (1024, 512), (1536, 512))
-OUT_CHUNKS = ((0, 0, 5), (1, 0, 5), (0, 5, 3), (1, 5, 3))
+PART = 512
+IN_CHUNKS = ((0, 0), (0, 2 * PART), (1, 0), (1, 2 * PART))
+BLK_FAR, BLK_MID, BLK_NEAR, BLK_OWN = (0, 3), (3, 5), (5, 7), (7, 8)
+OUT_CHUNKS = tuple(
+    ((a, lo * BLK, (hi - lo) * BLK // 2), (a, (lo + hi) * BLK // 2, (hi - lo) * BLK // 2))
+    for lo, hi in (BLK_FAR, BLK_MID, BLK_NEAR)
+    for a in (0, 1)
+) + (((0, 7 * BLK, BLK), (1, 7 * BLK, BLK)),)
+OUT_BLOCKS = tuple(((a, lo, hi),) for lo, hi in (BLK_FAR, BLK_MID, BLK_NEAR) for a in (0, 1)) + (
+    ((0, 7, 8), (1, 7, 8)),
+)
 NN = (((1,), (0,)), ((), ()))
 NT = (((1,), (1,)), ((), ()))
 TN = (((0,), (0,)), ((), ()))
@@ -33,9 +42,9 @@
 
 
 def kernel(
-    tok, ids, gates, gout, wgu_in, wd_in,
-    mixed_o, gtok_o, gg_o, gwgu_o, gwd_o,
-    wgu, wd, send, mid, fin, rmid, rfin, rows2, act, dpre, pre, dact, onehot, comb,
+    tok_in, ids, gates, gout_in, wgu_in, wd_in,
+    mixed_o, gtok_o, gwgu_o, gwd_o, gg_o,
+    tok, gout, wgu, wd, send, mid, fin, rmid, rfin, rows2, act, dpre, pre, dact, onehot, comb,
     terms, zpart, zs, zr, gsend, gin, gst_gu, gst_d,
     w_ls, w_ss, w_rs, a_ss, a_rs, a_ls, p_ss, p_rs, z_ss, z_rs, g_ss, g_rs, o_s,
 ):
@@ -53,21 +62,6 @@
         return pltpu.make_async_remote_copy(
             src_ref=src, dst_ref=dst, send_sem=ss, recv_sem=rs, device_id=to, device_id_type=MESH
         )
-
-    w_local = [
-        pltpu.make_async_copy(wgu_in.at[0], wgu.at[c], w_ls.at[0]),
-        pltpu.make_async_copy(wd_in.at[0], wd.at[c], w_ls.at[1]),
-    ]
-    for cp in w_local:
-        cp.start()
-    w_out = [
-        remote(wgu_in.at[0], wgu.at[c], w_ss.at[0], w_rs.at[0], other),
-        remote(wd_in.at[0], wd.at[c], w_ss.at[1], w_rs.at[1], other),
-    ]
-    w_come = [
-        remote(wgu_in.at[0], wgu.at[1 - c], w_ss.at[0], w_rs.at[0], other),
-        remote(wd_in.at[0], wd.at[1 - c], w_ss.at[1], w_rs.at[1], other),
-    ]
 
     barrier = pltpu.get_barrier_semaphore()
     peers = [dev(z, (x + d) % NX, y, c) for d in OFFS]
@@ -76,6 +70,28 @@
     peers += [other]
     for peer in peers:
         pl.semaphore_signal(barrier, inc=1, device_id=peer, device_id_type=MESH)
+
+    row_loads = [
+        pltpu.make_async_copy(tok_in, tok, w_ls.at[2]),
+        pltpu.make_async_copy(gout_in, gout, w_ls.at[3]),
+    ]
+    for cp in row_loads:
+        cp.start()
+
+    w_local = [
+        pltpu.make_async_copy(wgu_in.at[0], wgu.at[c], w_ls.at[0]),
+        pltpu.make_async_copy(wd_in.at[0], wd.at[c], w_ls.at[1]),
+    ]
+    for cp in w_local:
+        cp.start()
+    w_out = [
+        remote(wgu_in.at[0], wgu.at[c], w_ss.at[0], w_rs.at[0], other),
+        remote(wd_in.at[0], wd.at[c], w_ss.at[1], w_rs.at[1], other),
+    ]
+    w_come = [
+        remote(wgu_in.at[0], wgu.at[1 - c], w_ss.at[0], w_rs.at[0], other),
+        remote(wd_in.at[0], wd.at[1 - c], w_ss.at[1], w_rs.at[1], other),
+    ]
 
     local_ids = ids[...] - z * EXP
     hits, gate_rows = [], []
@@ -149,15 +165,21 @@
         return value.reshape(NX, NY, CAP, value.shape[-1]).astype(BF16)
 
     incoming = []
-    for n, cols in enumerate(IN_CHUNKS):
+    for n, (a, at) in enumerate(IN_CHUNKS):
         incoming.append(
-            [exchange(2 * n + a, send.at[a], mid.at[a], fin.at[a], cols, a == 0) for a in range(2)]
+            [
+                exchange(2 * n + i, send.at[a], mid.at[a], fin.at[a], (at + i * PART, PART), i == 0)
+                for i in range(2)
+            ]
         )
 
     def gather(n):
-        at, many = IN_CHUNKS[n]
-        send[0, :, :, :, at : at + many] = unstacked(dot(picks, tok[:, at : at + many]))
-        send[1, :, :, :, at : at + many] = unstacked(dot(picks, gout[:, at : at + many]) * slot_gate)
+        a, at = IN_CHUNKS[n]
+        cols = slice(at, at + 2 * PART)
+        if a == 0:
+            send[a, :, :, :, cols] = unstacked(dot(picks, tok[:, cols]))
+        else:
+            send[a, :, :, :, cols] = unstacked(dot(picks, gout[:, cols]) * slot_gate)
 
     def begin(n):
         for ex in incoming[n]:
@@ -168,33 +190,41 @@
             ex["forward"]()
 
     def first_part(n):
-        at, many = IN_CHUNKS[n]
-        for ex in incoming[n]:
+        a, at = IN_CHUNKS[n]
+        cols = slice(at, at + 2 * PART)
+        for i, ex in enumerate(incoming[n]):
             ex["arrive"]()
-        for a in range(2):
-            rows2[a, pl.ds(own_rows, SLOTS), at : at + many] = stacked(fin[a, :, :, :, at : at + many])
+            piece = slice(at + i * PART, at + (i + 1) * PART)
+            rows2[a, pl.ds(own_rows, SLOTS), piece] = stacked(fin[a, :, :, :, piece])
 
         def half(h, carry):
-            new_pre = dot(rows2[0, pl.ds(own_rows, SLOTS), at : at + many], wgu[h, at : at + many, :])
-            new_dact = dot(rows2[1, pl.ds(own_rows, SLOTS), at : at + many], wd[h, :, at : at + many], NT)
-            if n > 0:
-                new_pre = new_pre + pre[h]
-                new_dact = new_dact + dact[h]
-            if n < len(IN_CHUNKS) - 1:
-                pre[h] = new_pre
-                dact[h] = new_dact
+            rows = rows2[a, pl.ds(own_rows, SLOTS), cols]
+            if a == 0:
+                total = dot(rows, wgu[h, cols, :])
+                if at == 0:
+                    pre[h] = total
+                else:
+                    total = total + pre[h]
+                    pre[h] = total
+                    g, u = total[:, :FFP], total[:, FFP:]
+                    act[h, pl.ds(own_rows, SLOTS), :] = (g * jax.nn.sigmoid(g) * u).astype(BF16)
             else:
-                g, u = new_pre[:, :FFP], new_pre[:, FFP:]
-                sigma = jax.nn.sigmoid(g)
-                act[h, pl.ds(own_rows, SLOTS), :] = (g * sigma * u).astype(BF16)
-                dpre[h, pl.ds(own_rows, SLOTS), :FFP] = (
-                    new_dact * u * sigma * (1.0 + g * (1.0 - sigma))
-                ).astype(BF16)
-                dpre[h, pl.ds(own_rows, SLOTS), FFP:] = (new_dact * g * sigma).astype(BF16)
+                total = dot(rows, wd[h, :, cols], NT)
+                if at == 0:
+                    dact[h] = total
+                else:
+                    total = total + dact[h]
+                    g, u = pre[h, :, :FFP], pre[h, :, FFP:]
+                    sigma = jax.nn.sigmoid(g)
+                    dpre[h, pl.ds(own_rows, SLOTS), :FFP] = (
+                        total * u * sigma * (1.0 + g * (1.0 - sigma))
+                    ).astype(BF16)
+                    dpre[h, pl.ds(own_rows, SLOTS), FFP:] = (total * g * sigma).astype(BF16)
             return carry
 
         lax.fori_loop(0, 2, half, 0)
 
+    row_loads[0].wait()
     gather(0)
     pl.semaphore_wait(barrier, len(peers))
     begin(0)
@@ -202,27 +232,25 @@
         cp.start()
     gather(1)
     begin(1)
+    row_loads[1].wait()
     gather(2)
     forward_in(0)
     begin(2)
     gather(3)
+    forward_in(1)
+    begin(3)
     comb[1] = onehot[...].T.astype(BF16)
     comb[0] = (onehot[...] * slot_gate).T.astype(BF16)
-    forward_in(1)
-    begin(3)
     for cp in w_local:
         cp.wait()
     for cp in w_come:
         cp.wait_recv()
+    first_part(0)
     forward_in(2)
-    first_part(0)
-    forward_in(3)
-    first_part(1)
-    first_part(2)
-    for pair in incoming:
+    for pair in incoming[:2]:
         for ex in pair:
             ex["sent1"]()
-    first_part(3)
+    first_part(1)
 
     pushes = [
         (rows2.at[0], own_rows),
@@ -242,13 +270,11 @@
     ]
 
     outgoing = []
-    for n, (a, at, many) in enumerate(OUT_CHUNKS):
-        half = many * BLK // 2
-        base = 8 + 2 * n
+    for n, halves in enumerate(OUT_CHUNKS):
         outgoing.append(
             [
-                exchange(base + i, send.at[a], rmid.at[a], rfin.at[a], (at * BLK + i * half, half), i == 0)
-                for i in range(2)
+                exchange(8 + 2 * n + i, send.at[a], rmid.at[a], rfin.at[a], (at, many), i == 0)
+                for i, (a, at, many) in enumerate(halves)
             ]
         )
 
@@ -256,20 +282,20 @@
         return pl.multiple_of(((z + ring_step(pos) + NZ) % NZ) * BLK, BLK)
 
     def second_part(n):
-        a, at, many = OUT_CHUNKS[n]
-
-        def block(pos, carry):
-            j = plane_cols(pos)
-            if a == 0:
-                total = dot(act[0, pl.ds(own_rows, SLOTS), :], wd[0, :, pl.ds(j, BLK)])
-                total += dot(act[1, pl.ds(own_rows, SLOTS), :], wd[1, :, pl.ds(j, BLK)])
-            else:
-                total = dot(dpre[0, pl.ds(own_rows, SLOTS), :], wgu[0, pl.ds(j, BLK), :], NT)
-                total += dot(dpre[1, pl.ds(own_rows, SLOTS), :], wgu[1, pl.ds(j, BLK), :], NT)
-            send[a, :, :, :, pl.ds(pl.multiple_of(pos * BLK, BLK), BLK)] = unstacked(total)
-            return carry
-
-        lax.fori_loop(at, at + many, block, 0)
+        for a, lo, hi in OUT_BLOCKS[n]:
+
+            def block(pos, carry):
+                j = plane_cols(pos)
+                if a == 0:
+                    total = dot(act[0, pl.ds(own_rows, SLOTS), :], wd[0, :, pl.ds(j, BLK)])
+                    total += dot(act[1, pl.ds(own_rows, SLOTS), :], wd[1, :, pl.ds(j, BLK)])
+                else:
+                    total = dot(dpre[0, pl.ds(own_rows, SLOTS), :], wgu[0, pl.ds(j, BLK), :], NT)
+                    total += dot(dpre[1, pl.ds(own_rows, SLOTS), :], wgu[1, pl.ds(j, BLK), :], NT)
+                send[a, :, :, :, pl.ds(pl.multiple_of(pos * BLK, BLK), BLK)] = unstacked(total)
+                return carry
+
+            lax.fori_loop(lo, hi, block, 0)
         for ex in outgoing[n]:
             ex["start"]()
 
@@ -277,28 +303,31 @@
         for ex in outgoing[n]:
             ex["forward"]()
 
+    def block_sum(a, pos):
+        r = stacked(rfin[a, :, :, :, pl.ds(pl.multiple_of(pos * BLK, BLK), BLK)])
+        zpart[a, pos] = dot(comb[a], r)
+        if a == 0:
+            terms[...] += dot(r, gout[:, pl.ds(plane_cols(pos), BLK)], NT)
+
     def combine(n):
-        a, at, many = OUT_CHUNKS[n]
         for ex in outgoing[n]:
             ex["arrive"]()
-
-        def block(pos, carry):
-            r = stacked(rfin[a, :, :, :, pl.ds(pl.multiple_of(pos * BLK, BLK), BLK)])
-            zpart[a, pos] = dot(comb[a], r)
-            if a == 0:
-                terms[...] += dot(r, gout[:, pl.ds(plane_cols(pos), BLK)], NT)
-            return carry
-
-        lax.fori_loop(at, at + many, block, 0)
-
-    ring_pos = (0, 1, 3, 5, 2, 4, 6)
+        for a, lo, hi in OUT_BLOCKS[n]:
+
+            def block(pos, carry):
+                block_sum(a, pos)
+                return carry
+
+            lax.fori_loop(lo, hi, block, 0)
+
+    ring_pos = ((0, 1, 3, 5, 2, 4, 6), (0, 2, 4, 6, 1, 3, 5))
 
     def ring_copy(a, m):
-        to = dev((z + (1 if m < 4 else NZ - 1)) % NZ, x, y, c)
+        to = dev((z + (1 if (m < 4) == (a == 0) else NZ - 1)) % NZ, x, y, c)
         return remote(zs.at[a, m], zr.at[a, m], z_ss.at[a, m], z_rs.at[a, m], to)
 
     def ring(a, m):
-        total = zpart[a, ring_pos[m]]
+        total = zpart[a, ring_pos[a][m]]
         if m not in (0, 4):
             ring_copy(a, m - 1).wait_recv()
             total = total + zr[a, m - 1].astype(F32)
@@ -337,38 +366,57 @@
         out_copies.append(cp)
 
     second_part(0)
+    forward_in(3)
+    terms[...] = jnp.zeros_like(terms)
+    first_part(2)
+    for pair in incoming[2:]:
+        for ex in pair:
+            ex["sent1"]()
+    forward_out(0)
+    first_part(3)
     second_part(1)
     for cp in push_out:
         cp.start()
-    forward_out(0)
     second_part(2)
+    combine(0)
+    ring(0, 0)
+    ring(0, 4)
+    forward_out(1)
     second_part(3)
-    terms[...] = jnp.zeros_like(terms)
-    forward_out(1)
+    forward_out(2)
+    second_part(4)
+    ring(0, 1)
+    combine(1)
+    ring(1, 0)
+    ring(1, 4)
+    forward_out(3)
+    second_part(5)
+    combine(2)
+    ring(0, 2)
+    ring(0, 5)
+    forward_out(4)
+    second_part(6)
+    ring(1, 1)
     for cp in push_come:
         cp.wait_recv()
     grad_gu(0, 2)
-    combine(0)
-    ring(0, 0)
-    ring(0, 4)
-    forward_out(2)
+    combine(3)
+    ring(1, 2)
+    ring(1, 5)
+    forward_out(5)
     grad_gu(2, 4)
-    ring(0, 1)
-    ring(0, 5)
-    combine(1)
-    ring(1, 0)
-    ring(1, 4)
-    ring(0, 2)
-    forward_out(3)
-    grad_gu(4, 6)
-    ring(1, 1)
-    ring(1, 5)
-    grad_gu(6, 8)
-    ring(1, 2)
-    grad_d(0, 2)
-    combine(2)
+    combine(4)
     ring(0, 3)
     ring(0, 6)
+    forward_out(6)
+
+    grad_gu(4, 6)
+    combine(5)
+    ring(1, 3)
+    ring(1, 6)
+    grad_gu(6, 8)
+    grad_d(0, 4)
+    combine(6)
 
     kept = terms[...] * onehot[...]
     total = jnp.zeros((TOP, TOK), F32)
@@ -386,16 +434,12 @@
     for cp in g_out:
         cp.start()
     gin[z] = gsend[z]
-    grad_d(2, 4)
-
-    combine(3)
-    ring(1, 3)
-    ring(1, 6)
+
     ring_end(0, mixed_o)
+    ring_end(1, gtok_o)
     for cp in g_come:
         cp.wait_recv()
-    gg_o[...] = jnp.sum(gin[...], axis=0)
-    ring_end(1, gtok_o)
+    gg_o[...] = jnp.sum(gin[...], axis=0)[:1]
 
     for cp in w_out:
         cp.wait_send()
@@ -417,23 +461,52 @@
         cp.wait()
 
 
+def move(m_in, t_in, gu_in, d_in, g_in, m_out, t_out, gu_out, d_out, g_out, m, t, gu, d, sems):
+    trips = []
+    for src, via, dst, pieces in (
+        (gu_in.at[0], gu, gu_out.at[0], 8),
+        (d_in.at[0], d, d_out.at[0], 4),
+        (m_in, m, m_out, 1),
+        (t_in, t, t_out, 1),
+    ):
+        many = via.shape[0] // pieces
+        for i in range(pieces):
+            n, at = len(trips), pl.ds(i * many, many)
+            trips.append(
+                (
+                    pltpu.make_async_copy(src.at[at], via.at[at], sems.at[n, 0]),
+                    pltpu.make_async_copy(via.at[at], dst.at[at], sems.at[n, 1]),
+                )
+            )
+    for come, _ in trips:
+        come.start()
+    for come, leave in trips:
+        come.wait()
+        leave.start()
+    g_out[...] = g_in[...]
+    for _, leave in trips:
+        leave.wait()
+
+
 def local(tokens, expert_ids, gate_weights, grad_output, w_gate_up, w_down):
     vmem = pl.BlockSpec(memory_space=pltpu.VMEM)
     hbm = pl.BlockSpec(memory_space=pl.ANY)
     dma = pltpu.SemaphoreType.DMA
     quads = (2, NX, NY, CAP, WIDTH)
-    mixed, grad_tokens, gates, grad_gu, grad_dn = pl.pallas_call(
+    results = pl.pallas_call(
         kernel,
         out_shape=(
             jax.ShapeDtypeStruct((TOK, BLK), BF16),
             jax.ShapeDtypeStruct((TOK, BLK), BF16),
-            jax.ShapeDtypeStruct((8, TOK), F32),
             jax.ShapeDtypeStruct(w_gate_up.shape, BF16),
             jax.ShapeDtypeStruct(w_down.shape, BF16),
+            jax.ShapeDtypeStruct((1, TOK), F32),
         ),
-        in_specs=[vmem, vmem, vmem, vmem, hbm, hbm],
-        out_specs=(vmem, vmem, vmem, hbm, hbm),
+        in_specs=[hbm, vmem, vmem, hbm, hbm, hbm],
+        out_specs=(vmem, vmem, hbm, hbm, vmem),
         scratch_shapes=[
+            pltpu.VMEM((TOK, WIDTH), BF16),
+            pltpu.VMEM((TOK, WIDTH), BF16),
             pltpu.VMEM((2, WIDTH, 2 * FFP), BF16),
             pltpu.VMEM((2, FFP, WIDTH), BF16),
             pltpu.VMEM(quads, BF16),
@@ -456,8 +529,8 @@
             pltpu.VMEM((NZ, 8, TOK), F32),
             pltpu.VMEM((WIDTH, 2 * FFP), BF16),
             pltpu.VMEM((FFP, WIDTH), BF16),
-            dma((2,)), dma((2,)), dma((2,)),
-            dma((16, 6)), dma((16, 6)), dma((16, 2)),
+            dma((4,)), dma((2,)), dma((2,)),
+            dma((22, 6)), dma((22, 6)), dma((22, 2)),
             dma((4,)), dma((4,)),
             dma((2, 7)), dma((2, 7)),
             dma((7,)), dma((7,)),
@@ -468,7 +541,22 @@
         ),
         name="moe",
     )(tokens, expert_ids.T, gate_weights.T, grad_output, w_gate_up, w_down)
-    return mixed, grad_tokens, gates[:1].T, grad_gu, grad_dn
+    mixed, grad_tokens, grad_gu, grad_dn, gates = pl.pallas_call(
+        move,
+        out_shape=tuple(jax.ShapeDtypeStruct(r.shape, r.dtype) for r in results),
+        in_specs=[hbm] * 4 + [vmem],
+        out_specs=(hbm,) * 4 + (vmem,),
+        scratch_shapes=[
+            pltpu.VMEM((TOK, BLK), BF16),
+            pltpu.VMEM((TOK, BLK), BF16),
+            pltpu.VMEM((WIDTH, 2 * FFP), BF16),
+            pltpu.VMEM((FFP, WIDTH), BF16),
+            dma((14, 2)),
+        ],
+        compiler_params=pltpu.CompilerParams(vmem_limit_bytes=63 * 1024 * 1024),
+        name="move",
+    )(*results)
+    return mixed, grad_tokens, gates.T, grad_gu, grad_dn
 
 
 def solution(mesh):

time: 115 us -> 102 us (0.89)
  local copies, waits for them, and re-layouts: 9.41 us -> 0 us
  Pallas kernels: 105 us -> 101 us
    pallas_call x1, Pallas kernels: 105 us -> 95.4 us  [local(): pl.pallas_call(kernel, out_shape=(jax.ShapeDtypeStruct((TOK, BLK), BF16),...]
    unnamed x6 -> x0, local copies, waits for them, and re-layouts: 8.15 us -> none
    pallas_call x0 -> x1, Pallas kernels: none -> 5.64 us  [local(): pl.pallas_call(move, out_shape=tuple((jax.ShapeDtypeStruct(r.shape, r.dty...]
    transpose x1 -> x0, local copies, waits for them, and re-layouts: 1.26 us -> none  [local(): return (mixed, grad_tokens, gates[:1].T, grad_gu, grad_dn)]
where the time goes in v1:
time: 102 us
  Pallas kernels  101 us (99%)
    pallas_call x1, Pallas kernels, local(): pl.pallas_call(kernel, out_shape=(jax.ShapeDtypeStruct((TOK, BLK), BF16),...  95.4 us
    pallas_call x1, Pallas kernels, local(): pl.pallas_call(move, out_shape=tuple((jax.ShapeDtypeStruct(r.shape, r.dty...  5.64 us

profile of v1, /device:TPU:2, one launch (start us, length us, event | category | flops | bytes accessed | tf_op | source)
XLA Modules:
  0.0 101.7 jit_solution(4508597904492664111)
XLA Ops:
  0.6 95.4 %moe.1 = (bf16[256,256]{1,0:T(8,128)(2,1)}, bf16[256,256]{1,0:T(8,128)(2,1)}, bf16[1,2048,768]{2,1,0:T(8,128)(2,1)}, bf16[1,384,2048]{2,1,0:T(8,128)(2,1)}, f32[1,256]{1,0:T(1,128)}) custom-call(bf16[256,2048]{1,0:T(8,128)(2,1)} %tok_in.1, s32[8,256]{1,0:T(8,128)} %bitcast.3, f32[8,256]{1,0:T(8,128)} %bitcast.4, bf16[256,2048]{1,0:T(8,128)(2,1)} %gout_in.1, ...), custom_call_target="tpu_custom_call" | custom-call | tf_op jit(solution)/shard_map/moe/pallas_call | solution.py:496
  96.0 5.6 %move.1 = (bf16[256,256]{1,0:T(8,128)(2,1)}, bf16[256,256]{1,0:T(8,128)(2,1)}, bf16[1,2048,768]{2,1,0:T(8,128)(2,1)}, bf16[1,384,2048]{2,1,0:T(8,128)(2,1)}, f32[1,256]{1,0:T(1,128)}) custom-call(bf16[256,256]{1,0:T(8,128)(2,1)} %get-tuple-element.15.m_in, bf16[256,256]{1,0:T(8,128)(2,1)} %get-tuple-element.16.t_in, ...), custom_call_target="tpu_custom_call" | custom-call | tf_op jit(solution)/shard_map/move/pallas_call | solution.py:544

commit v2 on v1

--- a/solution.py
+++ b/solution.py
@@ -18,15 +18,11 @@
 BLK = WIDTH // NZ
 PART = 512
 IN_CHUNKS = ((0, 0), (0, 2 * PART), (1, 0), (1, 2 * PART))
-BLK_FAR, BLK_MID, BLK_NEAR, BLK_OWN = (0, 3), (3, 5), (5, 7), (7, 8)
+OUT_BLOCKS = ((0, 0, 5), (1, 0, 3), (0, 5, 8), (1, 3, 5), (1, 5, 8))
 OUT_CHUNKS = tuple(
-    ((a, lo * BLK, (hi - lo) * BLK // 2), (a, (lo + hi) * BLK // 2, (hi - lo) * BLK // 2))
-    for lo, hi in (BLK_FAR, BLK_MID, BLK_NEAR)
-    for a in (0, 1)
-) + (((0, 7 * BLK, BLK), (1, 7 * BLK, BLK)),)
-OUT_BLOCKS = tuple(((a, lo, hi),) for lo, hi in (BLK_FAR, BLK_MID, BLK_NEAR) for a in (0, 1)) + (
-    ((0, 7, 8), (1, 7, 8)),
+    ((a, lo * BLK, (hi - lo) * BLK // 2), (a, (lo + hi) * BLK // 2, (hi - lo) * BLK // 2)) for a, lo, hi in OUT_BLOCKS
 )
+PIECES = 2
 NN = (((1,), (0,)), ((), ()))
 NT = (((1,), (1,)), ((), ()))
 TN = (((0,), (0,)), ((), ()))
@@ -45,8 +41,8 @@
     tok_in, ids, gates, gout_in, wgu_in, wd_in,
     mixed_o, gtok_o, gwgu_o, gwd_o, gg_o,
     tok, gout, wgu, wd, send, mid, fin, rmid, rfin, rows2, act, dpre, pre, dact, onehot, comb,
-    terms, zpart, zs, zr, gsend, gin, gst_gu, gst_d,
-    w_ls, w_ss, w_rs, a_ss, a_rs, a_ls, p_ss, p_rs, z_ss, z_rs, g_ss, g_rs, o_s,
+    terms, zpart, zs, zr, gsend, gin,
+    w_ls, w_ss, w_rs, a_ss, a_rs, a_ls, p_ss, p_rs, z_ss, z_rs, g_ss, g_rs,
 ):
     z = lax.axis_index("tp")
     ep = lax.axis_index("ep")
@@ -250,6 +246,7 @@
     for pair in incoming[:2]:
         for ex in pair:
             ex["sent1"]()
+    forward_in(3)
     first_part(1)
 
     pushes = [
@@ -282,20 +279,22 @@
         return pl.multiple_of(((z + ring_step(pos) + NZ) % NZ) * BLK, BLK)
 
     def second_part(n):
-        for a, lo, hi in OUT_BLOCKS[n]:
-
-            def block(pos, carry):
-                j = plane_cols(pos)
-                if a == 0:
-                    total = dot(act[0, pl.ds(own_rows, SLOTS), :], wd[0, :, pl.ds(j, BLK)])
-                    total += dot(act[1, pl.ds(own_rows, SLOTS), :], wd[1, :, pl.ds(j, BLK)])
-                else:
-                    total = dot(dpre[0, pl.ds(own_rows, SLOTS), :], wgu[0, pl.ds(j, BLK), :], NT)
-                    total += dot(dpre[1, pl.ds(own_rows, SLOTS), :], wgu[1, pl.ds(j, BLK), :], NT)
-                send[a, :, :, :, pl.ds(pl.multiple_of(pos * BLK, BLK), BLK)] = unstacked(total)
-                return carry
-
-            lax.fori_loop(lo, hi, block, 0)
+        a, lo, hi = OUT_BLOCKS[n]
+
+        def block(pos, carry):
+            j = plane_cols(pos)
+            if a == 0:
+                total = dot(act[0, pl.ds(own_rows, SLOTS), :], wd[0, :, pl.ds(j, BLK)])
+                total += dot(act[1, pl.ds(own_rows, SLOTS), :], wd[1, :, pl.ds(j, BLK)])
+            else:
+                total = dot(dpre[0, pl.ds(own_rows, SLOTS), :], wgu[0, pl.ds(j, BLK), :], NT)
+                total += dot(dpre[1, pl.ds(own_rows, SLOTS), :], wgu[1, pl.ds(j, BLK), :], NT)
+            send[a, :, :, :, pl.ds(pl.multiple_of(pos * BLK, BLK), BLK)] = unstacked(total)
+            return carry
+
+        lax.fori_loop(lo, hi, block, 0)
+
+    def start_out(n):
         for ex in outgoing[n]:
             ex["start"]()
 
@@ -309,115 +308,104 @@
         if a == 0:
             terms[...] += dot(r, gout[:, pl.ds(plane_cols(pos), BLK)], NT)
 
-    def combine(n):
+    def arrive_out(n):
         for ex in outgoing[n]:
             ex["arrive"]()
-        for a, lo, hi in OUT_BLOCKS[n]:
-
-            def block(pos, carry):
-                block_sum(a, pos)
-                return carry
-
-            lax.fori_loop(lo, hi, block, 0)
+
+    def combine(n):
+        a, lo, hi = OUT_BLOCKS[n]
+        arrive_out(n)
+
+        def block(pos, carry):
+            block_sum(a, pos)
+            return carry
+
+        lax.fori_loop(lo, hi, block, 0)
 
     ring_pos = ((0, 1, 3, 5, 2, 4, 6), (0, 2, 4, 6, 1, 3, 5))
 
-    def ring_copy(a, m):
+    def ring_copy(a, m, piece):
         to = dev((z + (1 if (m < 4) == (a == 0) else NZ - 1)) % NZ, x, y, c)
-        return remote(zs.at[a, m], zr.at[a, m], z_ss.at[a, m], z_rs.at[a, m], to)
+        rows = pl.ds(piece * (TOK // PIECES), TOK // PIECES)
+        sems = (z_ss.at[a, m, piece], z_rs.at[a, m, piece])
+        return remote(zs.at[a, m, rows], zr.at[a, m, rows], *sems, to)
 
     def ring(a, m):
-        total = zpart[a, ring_pos[a][m]]
-        if m not in (0, 4):
-            ring_copy(a, m - 1).wait_recv()
-            total = total + zr[a, m - 1].astype(F32)
-        zs[a, m] = total.astype(BF16)
-        ring_copy(a, m).start()
+        for piece in range(PIECES):
+            rows = slice(piece * (TOK // PIECES), (piece + 1) * (TOK // PIECES))
+            total = zpart[a, ring_pos[a][m], rows]
+            if m not in (0, 4):
+                ring_copy(a, m - 1, piece).wait_recv()
+                total = total + zr[a, m - 1, rows].astype(F32)
+            zs[a, m, rows] = total.astype(BF16)
+            ring_copy(a, m, piece).start()
 
     def ring_end(a, out):
-        ring_copy(a, 3).wait_recv()
-        ring_copy(a, 6).wait_recv()
+        for piece in range(PIECES):
+            ring_copy(a, 3, piece).wait_recv()
+            ring_copy(a, 6, piece).wait_recv()
         out[...] = (zpart[a, 7] + zr[a, 3].astype(F32) + zr[a, 6].astype(F32)).astype(BF16)
-
-    out_copies = []
 
     def grad_gu(lo, hi):
         def tile(i, carry):
             cols = pl.ds(pl.multiple_of(i * 256, 256), 256)
-            gst_gu[cols, :] = dot(rows2[0, :, cols], dpre[c], TN).astype(BF16)
+            gwgu_o[0, cols, :] = dot(rows2[0, :, cols], dpre[c], TN).astype(BF16)
             return carry
 
         lax.fori_loop(lo, hi, tile, 0)
-        part = pl.ds(lo * 256, (hi - lo) * 256)
-        cp = pltpu.make_async_copy(gst_gu.at[part], gwgu_o.at[0, part], o_s.at[len(out_copies)])
-        cp.start()
-        out_copies.append(cp)
 
     def grad_d(lo, hi):
         def tile(i, carry):
             cols = pl.ds(pl.multiple_of(i * 512, 512), 512)
-            gst_d[:, cols] = dot(act[c], rows2[1, :, cols], TN).astype(BF16)
+            gwd_o[0, :, cols] = dot(act[c], rows2[1, :, cols], TN).astype(BF16)
             return carry
 
         lax.fori_loop(lo, hi, tile, 0)
-        part = pl.ds(lo * 512, (hi - lo) * 512)
-        cp = pltpu.make_async_copy(gst_d.at[:, part], gwd_o.at[0, :, part], o_s.at[len(out_copies)])
-        cp.start()
-        out_copies.append(cp)
 
     second_part(0)
-    forward_in(3)
+    start_out(0)
     terms[...] = jnp.zeros_like(terms)
     first_part(2)
+    second_part(2)
+    start_out(2)
+    forward_out(0)
     for pair in incoming[2:]:
         for ex in pair:
             ex["sent1"]()
-    forward_out(0)
     first_part(3)
     second_part(1)
+    start_out(1)
+    forward_out(2)
     for cp in push_out:
         cp.start()
-    second_part(2)
     combine(0)
     ring(0, 0)
     ring(0, 4)
+    second_part(3)
     forward_out(1)
-    second_part(3)
-    forward_out(2)
+    start_out(3)
     second_part(4)
+    start_out(4)
     ring(0, 1)
+    ring(0, 5)
+    combine(2)
+    forward_out(3)
     combine(1)
     ring(1, 0)
     ring(1, 4)
-    forward_out(3)
-    second_part(5)
-    combine(2)
     ring(0, 2)
-    ring(0, 5)
     forward_out(4)
-    second_part(6)
-    ring(1, 1)
     for cp in push_come:
         cp.wait_recv()
     grad_gu(0, 2)
+    ring(1, 1)
+    ring(0, 6)
+    ring(0, 3)
+    grad_gu(2, 3)
     combine(3)
     ring(1, 2)
     ring(1, 5)
-    forward_out(5)
-    grad_gu(2, 4)
-    combine(4)
-    ring(0, 3)
-    ring(0, 6)
-    forward_out(6)
-
-    grad_gu(4, 6)
-    combine(5)
-    ring(1, 3)
-    ring(1, 6)
-    grad_gu(6, 8)
-    grad_d(0, 4)
-    combine(6)
-
+    grad_gu(3, 5)
     kept = terms[...] * onehot[...]
     total = jnp.zeros((TOP, TOK), F32)
     for e in range(EXP):
@@ -435,11 +423,19 @@
         cp.start()
     gin[z] = gsend[z]
 
+    grad_gu(5, 8)
+    arrive_out(4)
+    block_sum(1, 5)
+    ring(1, 6)
+    block_sum(1, 6)
+    ring(1, 3)
+    block_sum(1, 7)
+    grad_d(0, 4)
     ring_end(0, mixed_o)
-    ring_end(1, gtok_o)
     for cp in g_come:
         cp.wait_recv()
     gg_o[...] = jnp.sum(gin[...], axis=0)[:1]
+    ring_end(1, gtok_o)
 
     for cp in w_out:
         cp.wait_send()
@@ -454,38 +450,29 @@
             ex["sent2"]()
     for a in range(2):
         for m in range(7):
-            ring_copy(a, m).wait_send()
+            for piece in range(PIECES):
+                ring_copy(a, m, piece).wait_send()
     for cp in g_out:
         cp.wait_send()
-    for cp in out_copies:
+
+
+def move(m_in, t_in, gu_in, d_in, g_in, m_out, t_out, gu_out, d_out, g_out, sems):
+    copies = []
+    for src, dst, pieces in (
+        (gu_in.at[0], gu_out.at[0], 4),
+        (d_in.at[0], d_out.at[0], 2),
+        (m_in, m_out, 1),
+        (t_in, t_out, 1),
+        (g_in, g_out, 1),
+    ):
+        many = src.shape[0] // pieces
+        for i in range(pieces):
+            at = pl.ds(i * many, many)
+            copies.append(pltpu.make_async_copy(src.at[at], dst.at[at], sems.at[len(copies)]))
+    for cp in copies:
+        cp.start()
+    for cp in copies:
         cp.wait()
-
-
-def move(m_in, t_in, gu_in, d_in, g_in, m_out, t_out, gu_out, d_out, g_out, m, t, gu, d, sems):
-    trips = []
-    for src, via, dst, pieces in (
-        (gu_in.at[0], gu, gu_out.at[0], 8),
-        (d_in.at[0], d, d_out.at[0], 4),
-        (m_in, m, m_out, 1),
-        (t_in, t, t_out, 1),
-    ):
-        many = via.shape[0] // pieces
-        for i in range(pieces):
-            n, at = len(trips), pl.ds(i * many, many)
-            trips.append(
-                (
-                    pltpu.make_async_copy(src.at[at], via.at[at], sems.at[n, 0]),
-                    pltpu.make_async_copy(via.at[at], dst.at[at], sems.at[n, 1]),
-                )
-            )
-    for come, _ in trips:
-        come.start()
-    for come, leave in trips:
-        come.wait()
-        leave.start()
-    g_out[...] = g_in[...]
-    for _, leave in trips:
-        leave.wait()
 
 
 def local(tokens, expert_ids, gate_weights, grad_output, w_gate_up, w_down):
@@ -496,14 +483,14 @@
     results = pl.pallas_call(
         kernel,
         out_shape=(
-            jax.ShapeDtypeStruct((TOK, BLK), BF16),
-            jax.ShapeDtypeStruct((TOK, BLK), BF16),
-            jax.ShapeDtypeStruct(w_gate_up.shape, BF16),
-            jax.ShapeDtypeStruct(w_down.shape, BF16),
-            jax.ShapeDtypeStruct((1, TOK), F32),
+            pltpu.VMEM((TOK, BLK), BF16),
+            pltpu.VMEM((TOK, BLK), BF16),
+            pltpu.VMEM(w_gate_up.shape, BF16),
+            pltpu.VMEM(w_down.shape, BF16),
+            pltpu.VMEM((1, TOK), F32),
         ),
         in_specs=[hbm, vmem, vmem, hbm, hbm, hbm],
-        out_specs=(vmem, vmem, hbm, hbm, vmem),
+        out_specs=(vmem,) * 5,
         scratch_shapes=[
             pltpu.VMEM((TOK, WIDTH), BF16),
             pltpu.VMEM((TOK, WIDTH), BF16),
@@ -527,33 +514,24 @@
             pltpu.VMEM((2, 7, TOK, BLK), BF16),
             pltpu.VMEM((TOP, 8, TOK), F32),
             pltpu.VMEM((NZ, 8, TOK), F32),
-            pltpu.VMEM((WIDTH, 2 * FFP), BF16),
-            pltpu.VMEM((FFP, WIDTH), BF16),
             dma((4,)), dma((2,)), dma((2,)),
-            dma((22, 6)), dma((22, 6)), dma((22, 2)),
+            dma((18, 6)), dma((18, 6)), dma((18, 2)),
             dma((4,)), dma((4,)),
-            dma((2, 7)), dma((2, 7)),
+            dma((2, 7, PIECES)), dma((2, 7, PIECES)),
             dma((7,)), dma((7,)),
-            dma((6,)),
         ],
         compiler_params=pltpu.CompilerParams(
-            collective_id=0, has_side_effects=True, vmem_limit_bytes=63 * 1024 * 1024
+            collective_id=0, has_side_effects=True, vmem_limit_bytes=54 * 1024 * 1024
         ),
         name="moe",
     )(tokens, expert_ids.T, gate_weights.T, grad_output, w_gate_up, w_down)
     mixed, grad_tokens, grad_gu, grad_dn, gates = pl.pallas_call(
         move,
         out_shape=tuple(jax.ShapeDtypeStruct(r.shape, r.dtype) for r in results),
-        in_specs=[hbm] * 4 + [vmem],
-        out_specs=(hbm,) * 4 + (vmem,),
-        scratch_shapes=[
-            pltpu.VMEM((TOK, BLK), BF16),
-            pltpu.VMEM((TOK, BLK), BF16),
-            pltpu.VMEM((WIDTH, 2 * FFP), BF16),
-            pltpu.VMEM((FFP, WIDTH), BF16),
-            dma((14, 2)),
-        ],
-        compiler_params=pltpu.CompilerParams(vmem_limit_bytes=63 * 1024 * 1024),
+        in_specs=[hbm] * 5,
+        out_specs=(hbm,) * 5,
+        scratch_shapes=[dma((9,))],
+        compiler_params=pltpu.CompilerParams(vmem_limit_bytes=2 * 1024 * 1024),
         name="move",
     )(*results)
     return mixed, grad_tokens, gates.T, grad_gu, grad_dn

time: 102 us -> 97.6 us (0.957)
  Pallas kernels: 101 us -> 96.4 us
    pallas_call x1, Pallas kernels: 5.64 us -> 2.33 us  [local(): pl.pallas_call(move, out_shape=tuple((jax.ShapeDtypeStruct(r.shape, r.dty...]
    pallas_call x1, Pallas kernels: 95.4 us -> 94.1 us  [local(): pl.pallas_call(kernel, out_shape=(pltpu.VMEM((TOK, BLK), BF16), pltpu.VME...]
where the time goes in v2:
time: 97.6 us; the launch traced here: 97.1 us
  Pallas kernels  96.4 us (99%)
    pallas_call x1, Pallas kernels, local(): pl.pallas_call(kernel, out_shape=(pltpu.VMEM((TOK, BLK), BF16), pltpu.VME...  94.1 us
    pallas_call x1, Pallas kernels, local(): pl.pallas_call(move, out_shape=tuple((jax.ShapeDtypeStruct(r.shape, r.dty...  2.33 us

profile of v2, /device:TPU:2, one launch (start us, length us, event | category | flops | bytes accessed | tf_op | source)
XLA Modules:
  0.0 97.1 jit_solution(17547245526793715882)
XLA Ops:
  0.6 94.1 %moe.1 = (bf16[256,256]{1,0:T(8,128)(2,1)S(1)}, bf16[256,256]{1,0:T(8,128)(2,1)S(1)}, bf16[1,2048,768]{2,1,0:T(8,128)(2,1)S(1)}, bf16[1,384,2048]{2,1,0:T(8,128)(2,1)S(1)}, f32[1,256]{1,0:T(1,128)S(1)}) custom-call(bf16[256,2048]{1,0:T(8,128)(2,1)} %tok_in.1, s32[8,256]{1,0:T(8,128)} %bitcast.3, f32[8,256]{1,0:T(8,128)} %bitcast.4, ...), custom_call_target="tpu_custom_call" | custom-call | tf_op jit(solution)/shard_map/moe/pallas_call | solution.py:483
  94.7 2.3 %move.1 = (bf16[256,256]{1,0:T(8,128)(2,1)}, bf16[256,256]{1,0:T(8,128)(2,1)}, bf16[1,2048,768]{2,1,0:T(8,128)(2,1)}, bf16[1,384,2048]{2,1,0:T(8,128)(2,1)}, f32[1,256]{1,0:T(1,128)}) custom-call(bf16[256,256]{1,0:T(8,128)(2,1)S(1)} %get-tuple-element.15.m_in, bf16[256,256]{1,0:T(8,128)(2,1)S(1)} %get-tuple-element.16.t_in, ...), custom_call_target="tpu_custom_call" | custom-call | tf_op jit(solution)/shard_map/move/pallas_call | solution.py:528

commit v3 on v2

--- a/solution.py
+++ b/solution.py
@@ -230,8 +230,8 @@
     begin(1)
     row_loads[1].wait()
     gather(2)
+    begin(2)
     forward_in(0)
-    begin(2)
     gather(3)
     forward_in(1)
     begin(3)

time: 97.6 us -> 97.7 us (level)
  no operation moved by 1% of the time
where the time goes in v3:
time: 97.7 us; the launch traced here: 97.1 us
  Pallas kernels  96.4 us (99%)
    pallas_call x1, Pallas kernels, local(): pl.pallas_call(kernel, out_shape=(pltpu.VMEM((TOK, BLK), BF16), pltpu.VME...  94.1 us
    pallas_call x1, Pallas kernels, local(): pl.pallas_call(move, out_shape=tuple((jax.ShapeDtypeStruct(r.shape, r.dty...  2.33 us

profile of v3, /device:TPU:2, one launch (start us, length us, event | category | flops | bytes accessed | tf_op | source)
XLA Modules:
  0.0 97.1 jit_solution(8674345855847802662)
XLA Ops:
  0.6 94.1 %moe.1 = (bf16[256,256]{1,0:T(8,128)(2,1)S(1)}, bf16[256,256]{1,0:T(8,128)(2,1)S(1)}, bf16[1,2048,768]{2,1,0:T(8,128)(2,1)S(1)}, bf16[1,384,2048]{2,1,0:T(8,128)(2,1)S(1)}, f32[1,256]{1,0:T(1,128)S(1)}) custom-call(bf16[256,2048]{1,0:T(8,128)(2,1)} %tok_in.1, s32[8,256]{1,0:T(8,128)} %bitcast.3, f32[8,256]{1,0:T(8,128)} %bitcast.4, ...), custom_call_target="tpu_custom_call" | custom-call | tf_op jit(solution)/shard_map/moe/pallas_call | solution.py:483
  94.7 2.3 %move.1 = (bf16[256,256]{1,0:T(8,128)(2,1)}, bf16[256,256]{1,0:T(8,128)(2,1)}, bf16[1,2048,768]{2,1,0:T(8,128)(2,1)}, bf16[1,384,2048]{2,1,0:T(8,128)(2,1)}, f32[1,256]{1,0:T(1,128)}) custom-call(bf16[256,256]{1,0:T(8,128)(2,1)S(1)} %get-tuple-element.15.m_in, bf16[256,256]{1,0:T(8,128)(2,1)S(1)} %get-tuple-element.16.t_in, ...), custom_call_target="tpu_custom_call" | custom-call | tf_op jit(solution)/shard_map/move/pallas_call | solution.py:528
